TPU v7x, 256 devices: a whole 4x4x8 slice. The times are simulated.
256 devices in a mesh: frames: 8 (over z_lo, x), dp: 32 (over y, z_hi, core).
Axes of the slice: x: 4, y: 4, z: 8 (z_hi: 4, z_lo: 2; z = z_hi * 2 + z_lo), core: 2. Of those that a mesh axis runs over, the one named last changes fastest.
Arguments:
- latents: bfloat16 [32, 16, 144, 640], P('dp', 'frames'), may hold values from -80 to 80
- pose: int32 [32, 16, 144], P('dp', 'frames'), may hold values from 0 to 18
- timesteps: int32 [32], P('dp'), may hold values from 0 to 999
- norm_gain: float32 [640], replicated, may hold values from 0.1 to 1.9
- norm_bias: float32 [640], replicated, may hold values from -0.5 to 0.5
- pose_table: float32 [19, 640], replicated, may hold values from -6 to 6
- time_weight: float32 [320, 640], replicated, may hold values from -0.3125 to 0.3125
- spatial_weight: bfloat16 [5760, 640], P('dp'), may hold values from -0.078125 to 0.078125
- temporal_weight: bfloat16 [1920, 640], P('dp'), may hold values from -0.125 to 0.125
- cotangent: bfloat16 [32, 16, 144, 640], P('dp', 'frames'), may hold values from -16 to 16
Outputs:
- mixed: float32 [32, 16, 144, 640], P('dp', 'frames')
- latent_grad: float32 [32, 16, 144, 640], P('dp', 'frames')
- temporal_grad: float32 [1920, 640], P('dp')
All inputs are finite; a program needn't handle non-finite values.
Results may differ from a plain program's by a relative error of at most 0.0053.
Values may be sent and summed in bfloat16 or wider, within the bound.
No kernel may reach another device: no remote copies, remote signals or barrier semaphores. Data moves between devices by JAX's collectives and lax.ppermute only.
A program may use at most 128 MiB of HBM per device.

v0:
```python
import math
import jax
import jax.numpy as jnp
from jax import lax
from jax.sharding import PartitionSpec as P

GROUP_CH = 40
HT = 9
WD = 16


def silu_slope(value):
    gate = jax.nn.sigmoid(value)
    return gate * (1.0 + value * (1.0 - gate))


def spatial_cols(field, sign):
    count_n, height, width, chans = field.shape
    padded = jnp.pad(field, ((0, 0), (1, 1), (1, 1), (0, 0)))
    pieces = []
    for row_tap in range(3):
        for col_tap in range(3):
            top = 1 + sign * (row_tap - 1)
            left = 1 + sign * (col_tap - 1)
            pieces.append(padded[:, top : top + height, left : left + width, :])
    return jnp.concatenate(pieces, axis=-1).reshape(count_n * height * width, 9 * chans)


def temporal_cols(extended, frame_span, sign):
    pieces = []
    for tap in range(3):
        begin = 1 + sign * (tap - 1)
        pieces.append(extended[:, begin : begin + frame_span])
    joined = jnp.concatenate(pieces, axis=-1)
    return joined.reshape(-1, joined.shape[-1])


def time_shift(timesteps, time_weight):
    half = time_weight.shape[0] // 2
    positions = jnp.arange(half, dtype=jnp.float32)
    frequencies = jnp.exp(-math.log(10000.0) * positions / half)
    angles = timesteps.astype(jnp.float32)[:, None] * frequencies[None, :]
    embedding = jnp.concatenate([jnp.cos(angles), jnp.sin(angles)], axis=-1)
    return jnp.dot(embedding, time_weight, precision=lax.Precision.HIGHEST)


def pose_rows(pose, pose_table):
    kinds = jnp.arange(pose_table.shape[0], dtype=jnp.int32)
    onehot = (pose[..., None] == kinds).astype(jnp.float32)
    return jnp.dot(onehot, pose_table, precision=lax.Precision.HIGHEST)


def pad_frames(field):
    return jnp.pad(field, ((0, 0), (1, 1), (0, 0), (0, 0)))


def per_device(
    latents,
    pose,
    timesteps,
    norm_gain,
    norm_bias,
    pose_table,
    time_weight,
    spatial_weight,
    temporal_weight,
    cotangent,
):
    clips_dev, frames_dev, pixels, chans = latents.shape
    groups = chans // GROUP_CH
    frames_all = frames_dev * lax.axis_size("frames")
    clips_all = clips_dev * lax.axis_size("dp")
    entries = float(pixels * GROUP_CH)
    row_count = clips_dev * frames_dev * pixels
    factor = 1.0 / math.sqrt(clips_all * frames_all * pixels)
    shifted = latents.astype(jnp.float32) + pose_rows(pose, pose_table)
    grouped = shifted.reshape(clips_dev, frames_dev, pixels, groups, GROUP_CH)
    center = jnp.sum(grouped, axis=(2, 4)) / entries
    variance = jnp.sum(grouped * grouped, axis=(2, 4)) / entries - center * center
    inv_std = lax.rsqrt(variance + 1e-05)[:, :, None, :, None]
    normed_g = (grouped - center[:, :, None, :, None]) * inv_std
    normed = normed_g.reshape(clips_dev, frames_dev, pixels, chans)
    before = normed * norm_gain + norm_bias
    activated = jax.nn.silu(before).astype(jnp.bfloat16)
    act_cols = spatial_cols(activated.reshape(clips_dev * frames_dev, HT, WD, chans), 1)
    columns = act_cols
    convolved = jnp.dot(
        columns,
        lax.all_gather(spatial_weight, "dp", axis=0, tiled=True),
        preferred_element_type=jnp.float32,
    )
    shifts = time_shift(timesteps, time_weight)
    spatial_out = (
        convolved.reshape(clips_dev, frames_dev, pixels, chans) + shifts[:, None, None, :]
    ).astype(jnp.bfloat16)
    local_out = lax.all_to_all(spatial_out, "frames", split_axis=2, concat_axis=1, tiled=True)
    extended = pad_frames(local_out)
    moved_ext = jax.nn.silu(extended.astype(jnp.float32)).astype(jnp.bfloat16)
    moved_cols = temporal_cols(moved_ext, frames_all, 1)
    columns = moved_cols
    temporal_out = jnp.dot(
        columns,
        lax.all_gather(temporal_weight, "dp", axis=0, tiled=True),
        preferred_element_type=jnp.float32,
    )
    local_mixed = local_out.astype(jnp.float32) + temporal_out.reshape(local_out.shape)
    mixed = lax.all_to_all(local_mixed, "frames", split_axis=1, concat_axis=2, tiled=True)
    grad_local = lax.all_to_all(cotangent, "frames", split_axis=2, concat_axis=1, tiled=True)
    grad_ext = pad_frames(grad_local)
    grad_cols = temporal_cols(grad_ext, frames_all, -1)
    temporal_back = lax.all_gather(temporal_weight, "dp", axis=0, tiled=True)
    back_moved = jnp.einsum(
        "rtc,tkc->rk",
        grad_cols.reshape(row_count, 3, chans),
        temporal_back.reshape(3, chans, chans),
        preferred_element_type=jnp.float32,
    )
    back_local = (
        grad_local.astype(jnp.float32)
        + back_moved.reshape(grad_local.shape) * silu_slope(local_out.astype(jnp.float32))
    ).astype(jnp.bfloat16)
    grad_flat = grad_local.reshape(row_count, chans)
    columns = moved_cols
    owned = lax.psum_scatter(
        lax.dot_general(
            columns, grad_flat, (((0,), (0,)), ((), ())), preferred_element_type=jnp.float32
        ),
        "dp",
        scatter_dimension=0,
        tiled=True,
    )
    temporal_grad = lax.psum(owned, "frames") * factor
    back_spatial = lax.all_to_all(back_local, "frames", split_axis=1, concat_axis=2, tiled=True)
    spatial_back = lax.all_gather(spatial_weight, "dp", axis=0, tiled=True)
    back_cols = spatial_cols(back_spatial.reshape(clips_dev * frames_dev, HT, WD, chans), -1)
    back_act = jnp.einsum(
        "rtc,tkc->rk",
        back_cols.reshape(row_count, 9, chans),
        spatial_back.reshape(9, chans, chans),
        preferred_element_type=jnp.float32,
    )
    back_normed = (
        back_act.reshape(clips_dev, frames_dev, pixels, chans) * silu_slope(before) * norm_gain
    )
    back_grouped = back_normed.reshape(clips_dev, frames_dev, pixels, groups, GROUP_CH)
    first_mean = (jnp.sum(back_grouped, axis=(2, 4)) / entries)[:, :, None, :, None]
    second_mean = (jnp.sum(back_grouped * normed_g, axis=(2, 4)) / entries)[:, :, None, :, None]
    latent_grad = inv_std * (back_grouped - first_mean - normed_g * second_mean)
    latent_grad = latent_grad.reshape(clips_dev, frames_dev, pixels, chans)
    return (mixed, latent_grad, temporal_grad)


def solution(mesh):
    placed = (
        P("dp", "frames", None, None),
        P("dp", "frames", None),
        P("dp"),
        P(),
        P(),
        P(),
        P(),
        P("dp", None),
        P("dp", None),
        P("dp", "frames", None, None),
    )
    return jax.shard_map(
        per_device,
        mesh=mesh,
        in_specs=placed,
        out_specs=(P("dp", "frames", None, None), P("dp", "frames", None, None), P("dp", None)),
        check_vma=False,
    )
```

profile of v0, /device:TPU:2, one launch (start us, length us, event | category | flops | bytes accessed | tf_op | source)
XLA Modules:
  0.0 397.9 jit_solution(13264229665452093458)
XLA Ops:
  8.7 2.0 copy.100
  10.7 6.2 %all-to-all-start.2 = ((bf16[1,2,144,640]{3,1,0,2:T(2,128)(2,1)}), bf16[1,2,144,640]{3,1,0,2:T(2,128)(2,1)S(1)}, u32[]{:S(2)}, u32[]{:S(2)}) async-start(bf16[1,2,144,640]{3,1,0,2:T(2,128)(2,1)} %copy.100), calls=%async_computation.2 | async-start | bytes 737280 | tf_op jit(solution)/shard_map/all_to_all | solution.py:108
  16.9 1.6 fusion.74
  24.0 1.7 copy-done.11
  26.3 59.8 %all-gather.5.cloned.1.call-done = bf16[32,180,640]{2,1,0:T(8,128)(2,1)} async-done(((bf16[1,180,640]{2,1,0:T(8,128)(2,1)}), bf16[32,180,640]{2,1,0:T(8,128)(2,1)}) %all-gather.5.cloned.1.call-update) | async-done | bytes 7372816 | tf_op jit(solution)/shard_map/all_gather | solution.py:89
  86.1 8.8 %reshape.259 = bf16[5760,640,1]{1,0,2:T(8,128)(2,1)} reshape(bf16[32,180,640]{2,1,0:T(8,128)(2,1)} %all-gather.5.cloned.1.call-done) | data formatting | bytes 14745600
  94.9 7.0 %fusion.50 = bf16[1,2,144,640]{3,2,1,0:T(8,128)(2,1)S(1)} fusion(bf16[2,144,5760]{2,1,0:T(8,128)(2,1)} %copy-done.11, bf16[5760,640,1]{1,0,2:T(8,128)(2,1)} %reshape.259, f32[640]{0:T(1024)S(1)} %convolution_reduce_fusion), kind=kOutput, calls=%fused_computation.24 | convolution fusion | flops 2123735040 | bytes 11061760 | tf_op jit(solution)/shard_map/dot_general | solution.py:87
  102.9 7.0 %all-to-all-start = ((bf16[1,2,144,640]{3,1,0,2:T(2,128)(2,1)}), bf16[1,2,144,640]{3,1,0,2:T(2,128)(2,1)S(1)}, u32[]{:S(2)}, u32[]{:S(2)}) async-start(bf16[1,2,144,640]{3,1,0,2:T(2,128)(2,1)} %copy.92), calls=%async_computation | async-start | bytes 737280 | tf_op jit(solution)/shard_map/all_to_all | solution.py:96
  112.1 1.9 reshape_reshape.6
  114.9 30.0 %all-gather.7.cloned.1.call-done = bf16[32,60,640]{2,1,0:T(8,128)(2,1)} async-done(((bf16[1,60,640]{2,1,0:T(8,128)(2,1)}), bf16[32,60,640]{2,1,0:T(8,128)(2,1)}) %all-gather.7.cloned.1.call-update) | async-done | bytes 2457616 | tf_op jit(solution)/shard_map/all_gather | solution.py:103
  144.9 4.1 %reshape.262 = bf16[1920,640,1]{1,0,2:T(8,128)(2,1)} reshape(bf16[32,60,640]{2,1,0:T(8,128)(2,1)} %all-gather.7.cloned.1.call-done) | data formatting | bytes 4915200
  149.0 4.1 %reshape.263 = bf16[3,640,640,1]{2,1,0,3:T(8,128)(2,1)} reshape(bf16[32,60,640]{2,1,0:T(8,128)(2,1)} %all-gather.7.cloned.1.call-done) | data formatting | bytes 4915200 | tf_op jit(solution)/shard_map/reshape | solution.py:115
  153.1 8.8 %reshape.265 = bf16[9,640,640,1]{2,1,0,3:T(8,128)(2,1)} reshape(bf16[32,180,640]{2,1,0:T(8,128)(2,1)} %all-gather.5.cloned.1.call-done) | data formatting | bytes 14745600 | tf_op jit(solution)/shard_map/reshape | solution.py:139
  164.8 1.5 reshape.248
  166.3 3.8 fusion.76
  170.1 98.5 %fusion = f32[64,640]{1,0:T(8,128)S(1)} fusion(f32[1920,640]{1,0:T(8,128)} %fusion.76), kind=kCustom, calls=%all-reduce-scatter | all-reduce-scatter fusion | flops 1310721 | bytes 5080064
  268.6 2.2 collective-permute-start
  271.3 2.0 collective-permute-start.1
  273.3 3.6 fusion.45
  276.9 4.1 %all-to-all-start.3 = ((bf16[1,16,18,640]{3,2,0,1:T(8,128)(2,1)}), bf16[1,16,18,640]{3,2,0,1:T(8,128)(2,1)}, u32[]{:S(2)}, u32[]{:S(2)}) async-start(bf16[1,16,18,640]{3,2,0,1:T(8,128)(2,1)} %fusion.45), calls=%async_computation.3 | async-start | bytes 983040 | tf_op jit(solution)/shard_map/all_to_all | solution.py:133
  281.1 4.7 %concatenate.49 = f32[188,640]{1,0:T(8,128)} concatenate(f32[60,640]{1,0:T(8,128)} %collective-permute-done.1, f32[64,640]{1,0:T(8,128)} %collective-permute-done, f32[64,640]{1,0:T(8,128)S(1)} %fusion), dimensions={0} | concatenate | bytes 962560
  285.7 1.6 constant_dynamic-slice_fusion
  287.4 3.1 fusion.26
  290.5 1.6 copy.98
  292.2 66.7 %all-reduce.8.cloned.1.call-done = f32[60,640]{1,0:T(8,128)} async-done(((f32[60,640]{1,0:T(8,128)}), f32[60,640]{1,0:T(8,128)}) %all-reduce.8.cloned.1.call-update) | async-done | bytes 153616 | tf_op jit(solution)/shard_map/psum | solution.py:132
  358.8 1.6 broadcast_multiply_fusion
  360.4 4.6 %all-to-all-start.1 = ((f32[1,16,18,640]{3,0,2,1:T(1,128)}), f32[1,16,18,640]{3,0,2,1:T(1,128)S(1)}, u32[]{:S(2)}, u32[]{:S(2)}) async-start(f32[1,16,18,640]{3,0,2,1:T(1,128)} %copy.98), calls=%async_computation.1 | async-start | bytes 1474560 | tf_op jit(solution)/shard_map/all_to_all | solution.py:107
  365.1 1.3 copy.110
  369.6 2.0 copy.111
  371.6 7.2 %reshape_reshape.7 = bf16[288,9,640]{2,1,0:T(8,128)(2,1)} reshape(bf16[2,9,16,5760]{3,2,1,0:T(8,128)(2,1)} %copy.111) | data formatting | bytes 6635520 | tf_op jit(solution)/shard_map/reshape;reshape | solution.py:138
  378.8 3.4 copy.112
  382.2 6.1 %fusion.60 = (f32[2,640]{1,0:T(2,128)S(1)}, f32[2,144,640]{2,1,0:T(8,128)S(1)}) fusion(f32[1,2,144,640]{3,2,1,0:T(8,128)S(1)} %get-tuple-element.42, f32[2,640]{1,0:T(2,128)S(1)} %mul.161, f32[2,640]{1,0:T(2,128)S(1)} %sub.66, f32[640]{0:T(1024)S(1)} %copy-done.12, f32[640]{0:T(1024)S(1)} %copy-done.13, bf16[2,144,640,9]{2,1,0,3:T(8,128)(2,1)S(1)} %bitcast.165, ...), kind=kOutput, calls=%fused_computation.47 | convolution fusion | flops 2126498560 | bytes 12185600 | tf_op jit(solution)/shard_map/rtc,tkc->rk/dot_general | solution.py:136
  (103 shorter events, 19.7 us)
Async XLA Ops:
  7.2 18.6 %copy-start = (f32[320,640]{1,0:T(8,128)S(1)}, f32[320,640]{1,0:T(8,128)}, u32[]{:S(2)}) copy-start(f32[320,640]{1,0:T(8,128)} %param.16) | copy-start | bytes 2457604
  7.2 78.9 %all-gather.5.cloned.1.call-start = ((), (), s32[]{:S(2)}) async-start(), calls=%async_computation.5 | async-start | bytes 7772160 | tf_op jit(solution)/shard_map/all_gather | solution.py:89
  7.9 137.0 %all-gather.7.cloned.1.call-start = ((), (), s32[]{:S(2)}) async-start(), calls=%async_computation.6 | async-start | bytes 2703360 | tf_op jit(solution)/shard_map/all_gather | solution.py:103
  10.7 92.2 %all-to-all-start.2 = ((bf16[1,2,144,640]{3,1,0,2:T(2,128)(2,1)}), bf16[1,2,144,640]{3,1,0,2:T(2,128)(2,1)S(1)}, u32[]{:S(2)}, u32[]{:S(2)}) async-start(bf16[1,2,144,640]{3,1,0,2:T(2,128)(2,1)} %copy.100), calls=%async_computation.2 | async-start | bytes 737280 | tf_op jit(solution)/shard_map/all_to_all | solution.py:108
  22.8 0.7 copy-start.12
  22.8 0.7 copy-start.13
  24.0 1.7 copy-start.11
  102.9 59.0 %all-to-all-start = ((bf16[1,2,144,640]{3,1,0,2:T(2,128)(2,1)}), bf16[1,2,144,640]{3,1,0,2:T(2,128)(2,1)S(1)}, u32[]{:S(2)}, u32[]{:S(2)}) async-start(bf16[1,2,144,640]{3,1,0,2:T(2,128)(2,1)} %copy.92), calls=%async_computation | async-start | bytes 737280 | tf_op jit(solution)/shard_map/all_to_all | solution.py:96
  162.4 0.8 copy-start.3
  162.5 0.9 copy-start.5
  162.5 1.1 copy-start.7
  162.5 3.9 copy-start.10
  268.6 4.7 %copy-start.2 = (bf16[3,640,640,1]{2,1,0,3:T(8,128)(2,1)S(1)}, bf16[3,640,640,1]{2,1,0,3:T(8,128)(2,1)}, u32[]{:S(2)}) copy-start(bf16[3,640,640,1]{2,1,0,3:T(8,128)(2,1)} %reshape.263) | copy-start | bytes 7372804
  268.6 4.7 %copy-start.9 = (bf16[288,3,640]{2,1,0:T(4,128)(2,1)S(1)}, bf16[288,3,640]{2,1,0:T(4,128)(2,1)}, u32[]{:S(2)}) copy-start(bf16[288,3,640]{2,1,0:T(4,128)(2,1)} %reshape_reshape.6) | copy-start | bytes 3317764
  268.6 12.4 %collective-permute-start = (f32[64,640]{1,0:T(8,128)S(1)}, f32[64,640]{1,0:T(8,128)}, u32[]{:S(2)}, u32[]{:S(2)}) collective-permute-start(f32[64,640]{1,0:T(8,128)S(1)} %fusion), channel_id=1, source_target_pairs={{0,1},{1,2},{2,3},{3,4},{4,5},{5,6},{6,7},{7,8},{8,9},{9,10},{10,1... | collective-permute-start | bytes 491528
  271.3 9.7 %collective-permute-start.1 = (f32[60,640]{1,0:T(8,128)S(1)}, f32[60,640]{1,0:T(8,128)}, u32[]{:S(2)}, u32[]{:S(2)}) collective-permute-start(f32[60,640]{1,0:T(8,128)S(1)} %slice.90), channel_id=1, source_target_pairs={{0,2},{1,3},{2,4},{3,5},{4,6},{5,7},{6,8},{7,9},{8,10},{9,11},{10,... | collective-permute-start | bytes 460808
  273.3 14.1 %copy-start.4 = (bf16[1,16,18,640]{3,2,1,0:T(8,128)(2,1)S(1)}, bf16[1,16,18,640]{3,2,1,0:T(8,128)(2,1)}, u32[]{:S(2)}) copy-start(bf16[1,16,18,640]{3,2,1,0:T(8,128)(2,1)} %copy-done.3) | copy-start | bytes 1105924
  273.3 14.1 %copy-start.6 = (bf16[1,16,18,640]{3,2,1,0:T(8,128)(2,1)S(1)}, bf16[1,16,18,640]{3,2,1,0:T(8,128)(2,1)}, u32[]{:S(2)}) copy-start(bf16[1,16,18,640]{3,2,1,0:T(8,128)(2,1)} %copy-done.5) | copy-start | bytes 1105924
  273.3 14.1 %copy-start.8 = (bf16[1,16,18,640]{3,2,1,0:T(8,128)(2,1)S(1)}, bf16[1,16,18,640]{3,2,1,0:T(8,128)(2,1)}, u32[]{:S(2)}) copy-start(bf16[1,16,18,640]{3,2,1,0:T(8,128)(2,1)} %copy-done.7) | copy-start | bytes 1105924
  276.9 83.5 %all-to-all-start.3 = ((bf16[1,16,18,640]{3,2,0,1:T(8,128)(2,1)}), bf16[1,16,18,640]{3,2,0,1:T(8,128)(2,1)}, u32[]{:S(2)}, u32[]{:S(2)}) async-start(bf16[1,16,18,640]{3,2,0,1:T(8,128)(2,1)} %fusion.45), calls=%async_computation.3 | async-start | bytes 983040 | tf_op jit(solution)/shard_map/all_to_all | solution.py:133
  281.0 77.8 %all-reduce.8.cloned.1.call-start = ((), (), s32[]{:S(2)}) async-start(), calls=%async_computation.4 | async-start | bytes 327680 | tf_op jit(solution)/shard_map/psum | solution.py:132
  360.4 29.6 %all-to-all-start.1 = ((f32[1,16,18,640]{3,0,2,1:T(1,128)}), f32[1,16,18,640]{3,0,2,1:T(1,128)S(1)}, u32[]{:S(2)}, u32[]{:S(2)}) async-start(f32[1,16,18,640]{3,0,2,1:T(1,128)} %copy.98), calls=%async_computation.1 | async-start | bytes 1474560 | tf_op jit(solution)/shard_map/all_to_all | solution.py:107
  382.2 9.2 %copy-start.1 = (f32[320,640]{1,0:T(8,128)S(1)}, f32[320,640]{1,0:T(8,128)}, u32[]{:S(2)}) copy-start(f32[320,640]{1,0:T(8,128)} %param.16) | copy-start | bytes 2457604
Sparse Core Ops, SparseCore 0:
  10.6 75.4 all-gather.4
  88.6 56.2 all-gather.6
  287.5 71.3 all-reduce.7
where the time goes:
time: 400 us; the launch traced here: 398 us
  waiting for transfers between devices  158 us (40%)
  blocking collectives  98.5 us (25%)
  local copies, waits for them, and re-layouts  67.7 us (17%)
  starting transfers between devices  26.2 us (7%)
  matrix products  25.7 us (6%)
  between operations  15.6 us (4%)
  other arithmetic  6.41 us (2%)
    unnamed x1, blocking collectives  98.5 us
    psum x1, waiting for transfers between devices, per_device(): temporal_grad = lax.psum(owned, 'frames') * factor  66.7 us
    all_gather x1, waiting for transfers between devices, per_device(): lax.all_gather(spatial_weight, 'dp', axis=0, tiled=True)  59.8 us
    all_gather x1, waiting for transfers between devices, per_device(): lax.all_gather(temporal_weight, 'dp', axis=0, tiled=True)  30 us
    unnamed x51, local copies, waits for them, and re-layouts  29.5 us
    reshape x1, local copies, waits for them, and re-layouts, per_device(): spatial_back.reshape(9, chans, chans)  8.79 us
  transfers between devices with their start and end apart: 9, of which 3 were waited for; matrix products, arithmetic and copies ran while one was open for 22% of the time, Pallas kernels for 0%

commit v1 on v0

--- a/solution.py
+++ b/solution.py
@@ -129,7 +129,7 @@
         scatter_dimension=0,
         tiled=True,
     )
-    temporal_grad = lax.psum(owned, "frames") * factor
+    temporal_grad = jnp.sum(lax.all_gather(owned, "frames"), axis=0) * factor
     back_spatial = lax.all_to_all(back_local, "frames", split_axis=1, concat_axis=2, tiled=True)
     spatial_back = lax.all_gather(spatial_weight, "dp", axis=0, tiled=True)
     back_cols = spatial_cols(back_spatial.reshape(clips_dev * frames_dev, HT, WD, chans), -1)

time: 400 us -> 339 us (0.85)
  waiting for transfers between devices: 158 us -> 104 us
  local copies, waits for them, and re-layouts: 67.7 us -> 63.6 us
    psum x1 -> x0, waiting for transfers between devices: 66.7 us -> none  [per_device(): temporal_grad = lax.psum(owned, 'frames') * factor]
    all_gather x0 -> x1, waiting for transfers between devices: none -> 10.3 us  [per_device(): temporal_grad = jnp.sum(lax.all_gather(owned, 'frames'), axis=0) * factor]
    unnamed x51 -> x55, local copies, waits for them, and re-layouts: 29.5 us -> 25.7 us
  transfers between devices with their start and end apart: 9 -> 9, of which waited for: 3 -> 4; matrix products, arithmetic and copies ran while one was open for 22% -> 54% of each run, Pallas kernels for 0% -> 0%
where the time goes in v1:
time: 339 us; the launch traced here: 337 us
  waiting for transfers between devices  104 us (31%)
  blocking collectives  96.1 us (28%)
  local copies, waits for them, and re-layouts  63.6 us (19%)
  starting transfers between devices  25.6 us (8%)
  matrix products  24.5 us (7%)
  between operations  15.5 us (5%)
  other arithmetic  7.96 us (2%)
    unnamed x1, blocking collectives  96.1 us
    all_gather x1, waiting for transfers between devices, per_device(): lax.all_gather(spatial_weight, 'dp', axis=0, tiled=True)  59.8 us
    all_gather x1, waiting for transfers between devices, per_device(): lax.all_gather(temporal_weight, 'dp', axis=0, tiled=True)  30.1 us
    unnamed x55, local copies, waits for them, and re-layouts  25.7 us
    all_gather x1, waiting for transfers between devices, per_device(): temporal_grad = jnp.sum(lax.all_gather(owned, 'frames'), axis=0) * factor  10.3 us
    reshape x1, local copies, waits for them, and re-layouts, per_device(): spatial_back.reshape(9, chans, chans)  8.79 us
    another operation x1, local copies, waits for them, and re-layouts, per_device(): back_cols.reshape(row_count, 9, chans)  7.12 us
    all_to_all x1, starting transfers between devices, per_device(): lax.all_to_all(spatial_out, 'frames', split_axis=2, concat_axis=1, tiled=...  6.99 us
  transfers between devices with their start and end apart: 9, of which 4 were waited for; matrix products, arithmetic and copies ran while one was open for 54% of the time, Pallas kernels for 0%

profile of v1, /device:TPU:2, one launch (start us, length us, event | category | flops | bytes accessed | tf_op | source)
XLA Modules:
  0.0 337.2 jit_solution(14478877668573938220)
XLA Ops:
  8.7 2.0 copy.100
  10.7 6.2 %all-to-all-start.2 = ((bf16[1,2,144,640]{3,1,0,2:T(2,128)(2,1)}), bf16[1,2,144,640]{3,1,0,2:T(2,128)(2,1)S(1)}, u32[]{:S(2)}, u32[]{:S(2)}) async-start(bf16[1,2,144,640]{3,1,0,2:T(2,128)(2,1)} %copy.100), calls=%async_computation.2 | async-start | bytes 737280 | tf_op jit(solution)/shard_map/all_to_all | solution.py:108
  16.9 1.6 fusion.74
  19.9 1.3 dynamic-slice.4
  24.0 1.7 copy-done.13
  26.2 59.8 %all-gather.8.cloned.1.call-done = bf16[32,180,640]{2,1,0:T(8,128)(2,1)} async-done(((bf16[1,180,640]{2,1,0:T(8,128)(2,1)}), bf16[32,180,640]{2,1,0:T(8,128)(2,1)}) %all-gather.8.cloned.1.call-update) | async-done | bytes 7372816 | tf_op jit(solution)/shard_map/all_gather | solution.py:89
  86.1 8.8 %reshape.263 = bf16[5760,640,1]{1,0,2:T(8,128)(2,1)} reshape(bf16[32,180,640]{2,1,0:T(8,128)(2,1)} %all-gather.8.cloned.1.call-done) | data formatting | bytes 14745600
  94.9 6.9 %fusion.50 = bf16[1,2,144,640]{3,2,1,0:T(8,128)(2,1)S(1)} fusion(bf16[2,144,5760]{2,1,0:T(8,128)(2,1)} %copy-done.13, bf16[5760,640,1]{1,0,2:T(8,128)(2,1)} %reshape.263, f32[640]{0:T(1024)S(1)} %convolution_reduce_fusion), kind=kOutput, calls=%fused_computation.24 | convolution fusion | flops 2123735040 | bytes 11061760 | tf_op jit(solution)/shard_map/dot_general | solution.py:87
  102.8 7.0 %all-to-all-start = ((bf16[1,2,144,640]{3,1,0,2:T(2,128)(2,1)}), bf16[1,2,144,640]{3,1,0,2:T(2,128)(2,1)S(1)}, u32[]{:S(2)}, u32[]{:S(2)}) async-start(bf16[1,2,144,640]{3,1,0,2:T(2,128)(2,1)} %copy.92), calls=%async_computation | async-start | bytes 737280 | tf_op jit(solution)/shard_map/all_to_all | solution.py:96
  112.0 1.9 reshape_reshape.6
  114.8 30.1 %all-gather.10.cloned.1.call-done = bf16[32,60,640]{2,1,0:T(8,128)(2,1)} async-done(((bf16[1,60,640]{2,1,0:T(8,128)(2,1)}), bf16[32,60,640]{2,1,0:T(8,128)(2,1)}) %all-gather.10.cloned.1.call-update) | async-done | bytes 2457616 | tf_op jit(solution)/shard_map/all_gather | solution.py:103
  144.9 4.1 %reshape.266 = bf16[1920,640,1]{1,0,2:T(8,128)(2,1)} reshape(bf16[32,60,640]{2,1,0:T(8,128)(2,1)} %all-gather.10.cloned.1.call-done) | data formatting | bytes 4915200
  149.0 4.1 %reshape.267 = bf16[3,640,640,1]{2,1,0,3:T(8,128)(2,1)} reshape(bf16[32,60,640]{2,1,0:T(8,128)(2,1)} %all-gather.10.cloned.1.call-done) | data formatting | bytes 4915200 | tf_op jit(solution)/shard_map/reshape | solution.py:115
  153.1 8.8 %reshape.269 = bf16[9,640,640,1]{2,1,0,3:T(8,128)(2,1)} reshape(bf16[32,180,640]{2,1,0:T(8,128)(2,1)} %all-gather.8.cloned.1.call-done) | data formatting | bytes 14745600 | tf_op jit(solution)/shard_map/reshape | solution.py:139
  167.2 2.3 fusion.45
  169.4 4.9 %all-to-all-start.3 = ((bf16[1,16,18,640]{3,2,0,1:T(8,128)(2,1)}), bf16[1,16,18,640]{3,2,0,1:T(8,128)(2,1)S(1)}, u32[]{:S(2)}, u32[]{:S(2)}) async-start(bf16[1,16,18,640]{3,2,0,1:T(8,128)(2,1)} %fusion.45), calls=%async_computation.3 | async-start | bytes 983040 | tf_op jit(solution)/shard_map/all_to_all | solution.py:133
  174.4 1.3 pad_maximum_fusion
  175.7 1.5 reshape.248
  177.3 3.8 %fusion.76 = f32[1920,640]{1,0:T(8,128)} fusion(bf16[288,1920]{1,0:T(8,128)(2,1)S(1)} %reshape.248, bf16[288,640]{1,0:T(8,128)(2,1)S(1)} %copy-done.11), kind=kOutput, calls=%fused_computation.99 | convolution fusion | flops 707788800 | bytes 6389760 | tf_op jit(solution)/shard_map/dot_general | solution.py:125
  181.1 96.1 %fusion = f32[64,640]{1,0:T(8,128)S(1)} fusion(f32[1920,640]{1,0:T(8,128)} %fusion.76), kind=kCustom, calls=%all-reduce-scatter | all-reduce-scatter fusion | flops 1310721 | bytes 5080064
  277.2 1.3 collective-permute-start
  278.5 1.3 collective-permute-start.1
  279.8 3.4 %fusion.26 = f32[1,16,18,640]{3,2,1,0:T(8,128)S(1)} fusion(f32[16,18,640]{2,1,0:T(8,128)S(1)} %bitcast.166, bf16[1920,640,1]{1,0,2:T(8,128)(2,1)} %reshape.266, bf16[1,16,18,640]{3,2,1,0:T(8,128)(2,1)} %copy-done.7, bf16[1,16,18,640]{3,2,1,0:T(8,128)(2,1)} %get-tuple-element.25, bf16[1,16,18,640]{3,2,1,0:T(8,128)(2,1)S(1)} %copy-done.6), kind=kOutput, calls=%fused_computation.14 | convolution fusion | flops 711290880 | bytes 5038080 | tf_op jit(solution)/shard_map/dot_general | solution.py:101
  283.3 1.6 copy.98
  284.9 2.2 collective-permute-done.1
  288.3 4.8 %all-to-all-start.1 = ((f32[1,16,18,640]{3,0,2,1:T(1,128)}), f32[1,16,18,640]{3,0,2,1:T(1,128)S(1)}, u32[]{:S(2)}, u32[]{:S(2)}) async-start(f32[1,16,18,640]{3,0,2,1:T(1,128)} %copy.98), calls=%async_computation.1 | async-start | bytes 1474560 | tf_op jit(solution)/shard_map/all_to_all | solution.py:107
  296.5 2.0 copy.111
  298.5 7.1 %reshape_reshape.7 = bf16[288,9,640]{2,1,0:T(8,128)(2,1)} reshape(bf16[2,9,16,5760]{3,2,1,0:T(8,128)(2,1)} %copy.111) | data formatting | bytes 6635520 | tf_op jit(solution)/shard_map/reshape;reshape | solution.py:138
  305.7 3.4 %copy.112 = bf16[288,640,9]{1,0,2:T(8,128)(2,1)S(1)} copy(bf16[288,640,9]{1,2,0:T(8,128)(2,1)} %bitcast.165) | data formatting | bytes 6635520 | tf_op jit(solution)/shard_map/rtc,tkc->rk/dot_general | solution.py:136
  309.1 6.0 %fusion.60 = (f32[2,640]{1,0:T(2,128)S(1)}, f32[2,144,640]{2,1,0:T(8,128)S(1)}) fusion(f32[1,2,144,640]{3,2,1,0:T(8,128)S(1)} %get-tuple-element.42, f32[2,640]{1,0:T(2,128)S(1)} %mul.161, f32[2,640]{1,0:T(2,128)S(1)} %sub.66, f32[640]{0:T(1024)S(1)} %copy-done.14, f32[640]{0:T(1024)S(1)} %copy-done.15, bf16[2,144,640,9]{2,1,0,3:T(8,128)(2,1)S(1)} %bitcast.167, ...), kind=kOutput, calls=%fused_computation.47 | convolution fusion | flops 2126498560 | bytes 12185600 | tf_op jit(solution)/shard_map/rtc,tkc->rk/dot_general | solution.py:136
  318.2 10.3 %all-gather.12.cloned.1.call-done = f32[8,60,640]{2,1,0:T(8,128)} async-done(((f32[1,60,640]{2,1,0:T(8,128)}), f32[8,60,640]{2,1,0:T(8,128)}) %all-gather.12.cloned.1.call-update) | async-done | bytes 1228816 | tf_op jit(solution)/shard_map/all_gather | solution.py:132
  328.6 1.4 reduce_sum.85
  (108 shorter events, 22.4 us)
Async XLA Ops:
  7.2 18.5 %copy-start = (f32[320,640]{1,0:T(8,128)S(1)}, f32[320,640]{1,0:T(8,128)}, u32[]{:S(2)}) copy-start(f32[320,640]{1,0:T(8,128)} %param.16) | copy-start | bytes 2457604
  7.2 78.9 %all-gather.8.cloned.1.call-start = ((), (), s32[]{:S(2)}) async-start(), calls=%async_computation.4 | async-start | bytes 7772160 | tf_op jit(solution)/shard_map/all_gather | solution.py:89
  7.9 137.0 %all-gather.10.cloned.1.call-start = ((), (), s32[]{:S(2)}) async-start(), calls=%async_computation.5 | async-start | bytes 2703360 | tf_op jit(solution)/shard_map/all_gather | solution.py:103
  10.7 92.1 %all-to-all-start.2 = ((bf16[1,2,144,640]{3,1,0,2:T(2,128)(2,1)}), bf16[1,2,144,640]{3,1,0,2:T(2,128)(2,1)S(1)}, u32[]{:S(2)}, u32[]{:S(2)}) async-start(bf16[1,2,144,640]{3,1,0,2:T(2,128)(2,1)} %copy.100), calls=%async_computation.2 | async-start | bytes 737280 | tf_op jit(solution)/shard_map/all_to_all | solution.py:108
  22.8 0.7 copy-start.14
  22.8 0.7 copy-start.15
  24.0 1.7 copy-start.13
  102.8 59.1 %all-to-all-start = ((bf16[1,2,144,640]{3,1,0,2:T(2,128)(2,1)}), bf16[1,2,144,640]{3,1,0,2:T(2,128)(2,1)S(1)}, u32[]{:S(2)}, u32[]{:S(2)}) async-start(bf16[1,2,144,640]{3,1,0,2:T(2,128)(2,1)} %copy.92), calls=%async_computation | async-start | bytes 737280 | tf_op jit(solution)/shard_map/all_to_all | solution.py:96
  161.9 0.7 copy-start.10
  163.9 1.6 copy-start.2
  163.9 2.2 copy-start.4
  163.9 3.0 copy-start.9
  163.9 3.3 copy-start.12
  165.2 9.2 %copy-start.5 = (bf16[1,16,18,640]{3,2,1,0:T(8,128)(2,1)}, bf16[1,16,18,640]{3,2,1,0:T(8,128)(2,1)S(1)}, u32[]{:S(2)}) copy-start(bf16[1,16,18,640]{3,2,1,0:T(8,128)(2,1)S(1)} %get-tuple-element.23) | copy-start | bytes 1105924
  165.2 9.2 %copy-start.7 = (bf16[1,16,18,640]{3,2,1,0:T(8,128)(2,1)}, bf16[1,16,18,640]{3,2,1,0:T(8,128)(2,1)S(1)}, u32[]{:S(2)}) copy-start(bf16[1,16,18,640]{3,2,1,0:T(8,128)(2,1)S(1)} %get-tuple-element.24) | copy-start | bytes 1105924
  167.2 7.2 %copy-start.8 = (bf16[1,16,18,640]{3,2,1,0:T(8,128)(2,1)S(1)}, bf16[1,16,18,640]{3,2,1,0:T(8,128)(2,1)}, u32[]{:S(2)}) copy-start(bf16[1,16,18,640]{3,2,1,0:T(8,128)(2,1)} %get-tuple-element.25) | copy-start | bytes 1105924
  169.4 7.8 %copy-start.11 = (bf16[288,640]{1,0:T(8,128)(2,1)S(1)}, bf16[288,640]{1,0:T(8,128)(2,1)}, u32[]{:S(2)}) copy-start(bf16[288,640]{1,0:T(8,128)(2,1)} %reshape.249) | copy-start | bytes 1105924
  169.4 118.8 %all-to-all-start.3 = ((bf16[1,16,18,640]{3,2,0,1:T(8,128)(2,1)}), bf16[1,16,18,640]{3,2,0,1:T(8,128)(2,1)S(1)}, u32[]{:S(2)}, u32[]{:S(2)}) async-start(bf16[1,16,18,640]{3,2,0,1:T(8,128)(2,1)} %fusion.45), calls=%async_computation.3 | async-start | bytes 983040 | tf_op jit(solution)/shard_map/all_to_all | solution.py:133
  174.4 154.2 %all-gather.12.cloned.1.call-start = ((), (), s32[]{:S(2)}) async-start(), calls=%async_computation.6 | async-start | bytes 1474560 | tf_op jit(solution)/shard_map/all_gather | solution.py:132
  181.1 98.8 %copy-start.3 = (f32[1,8,2,18,640]{4,3,2,1,0:T(8,128)S(1)}, f32[1,8,2,18,640]{4,3,2,1,0:T(8,128)}, u32[]{:S(2)}) copy-start(f32[1,8,2,18,640]{4,3,2,1,0:T(8,128)} %copy-done.2) | copy-start | bytes 2211844
  181.1 98.8 %copy-start.6 = (bf16[1,16,18,640]{3,2,1,0:T(8,128)(2,1)S(1)}, bf16[1,16,18,640]{3,2,1,0:T(8,128)(2,1)}, u32[]{:S(2)}) copy-start(bf16[1,16,18,640]{3,2,1,0:T(8,128)(2,1)} %copy-done.5) | copy-start | bytes 1105924
  277.2 9.9 %collective-permute-start = (f32[64,640]{1,0:T(8,128)S(1)}, f32[64,640]{1,0:T(8,128)S(1)}, u32[]{:S(2)}, u32[]{:S(2)}) collective-permute-start(f32[64,640]{1,0:T(8,128)S(1)} %fusion), channel_id=1, source_target_pairs={{0,1},{1,2},{2,3},{3,4},{4,5},{5,6},{6,7},{7,8},{8,9},{9,10},{10,1... | collective-permute-start | bytes 491528
  278.5 8.6 %collective-permute-start.1 = (f32[60,640]{1,0:T(8,128)S(1)}, f32[60,640]{1,0:T(8,128)S(1)}, u32[]{:S(2)}, u32[]{:S(2)}) collective-permute-start(f32[60,640]{1,0:T(8,128)S(1)} %slice.90), channel_id=1, source_target_pairs={{0,2},{1,3},{2,4},{3,5},{4,6},{5,7},{6,8},{7,9},{8,10},{9,11},{10,... | collective-permute-start | bytes 460808
  288.3 28.7 %all-to-all-start.1 = ((f32[1,16,18,640]{3,0,2,1:T(1,128)}), f32[1,16,18,640]{3,0,2,1:T(1,128)S(1)}, u32[]{:S(2)}, u32[]{:S(2)}) async-start(f32[1,16,18,640]{3,0,2,1:T(1,128)} %copy.98), calls=%async_computation.1 | async-start | bytes 1474560 | tf_op jit(solution)/shard_map/all_to_all | solution.py:107
  315.8 14.8 %copy-start.1 = (f32[320,640]{1,0:T(8,128)S(1)}, f32[320,640]{1,0:T(8,128)}, u32[]{:S(2)}) copy-start(f32[320,640]{1,0:T(8,128)} %param.16) | copy-start | bytes 2457604
Sparse Core Ops, SparseCore 0:
  10.6 75.4 all-gather.7
  88.6 56.2 all-gather.9
  288.4 40.1 all-gather.11
